TPU v7x, 32 devices: a whole 2x2x4 slice. The times are simulated.
32 devices in a mesh: rows: 8 (over z, y), cols: 4 (over x, core).
Axes of the slice: x: 2, y: 2, z: 4, core: 2. Of those that a mesh axis runs over, the one named last changes fastest.
Arguments:
- z_blocks: float32 [32, 4, 256, 256], P('rows', 'cols'), may hold values from -0.1875 to 0.1875
- z_cols: int32 [32, 4], P('rows', 'cols'), may hold values from 0 to 31, as said below
- z_count: int32 [32], P('rows'), may hold values from 1 to 4, as said below
- h_blocks: float32 [32, 4, 256, 256], P('rows', 'cols'), may hold values from -0.1875 to 0.1875
- h_cols: int32 [32, 4], P('rows', 'cols'), may hold values from 0 to 31, as said below
- h_count: int32 [32], P('rows'), may hold values from 1 to 4, as said below
- panel: float32 [32, 256, 64], P('rows'), may hold values from -6 to 6
Outputs:
- result: float32 [32, 256, 64], P('rows', 'cols')
Inputs may be any that keep to these rules, and one draw needn't show every extreme that they name: `z_cols`: within a block row the column block indices of the slots are distinct; block row i only names blocks from 4 * (i // 4) - 4 to 4 * (i // 4) + 7. `h_cols`: same law as z_cols, drawn apart. `z_count`: block row 0 uses all 4 slots. `h_count`: block row 0 uses all 4 slots.
All inputs are finite; a program needn't handle non-finite values.
Results may differ from a plain program's by a relative error of at most 0.000098.
Values sent between devices are 32-bit elements; how exact they have to be, the bound alone decides.
A program may use at most 64 MiB of HBM per device.

v0:
```python
import jax
import jax.numpy as jnp
from jax import lax
from jax.sharding import PartitionSpec as P

HB = 4


def with_halo(block, sides, width):
    for axis, dim in sides:
        count = lax.axis_size(axis)
        forward = [(i, i + 1) for i in range(count - 1)]
        backward = [(target, source) for source, target in forward]
        low = lax.ppermute(
            lax.slice_in_dim(block, block.shape[dim] - width, None, axis=dim), axis, forward
        )
        high = lax.ppermute(lax.slice_in_dim(block, 0, width, axis=dim), axis, backward)
        block = jnp.concatenate([low, block, high], axis=dim)
    return block


def slot_mask(count, slots):
    first = lax.axis_index("cols") * slots
    return (first + jnp.arange(slots)[None, :] < count[:, None]).astype(jnp.float32)


def window_start(own_rows):
    return lax.axis_index("rows") * own_rows - HB


def share_window(share):
    arrived = with_halo(share, (("rows", 0),), HB)
    return lax.all_gather(arrived, "cols", axis=2, tiled=True)


def contract(blocks, cols, count, window, own_rows):
    offsets = cols - window_start(own_rows)
    picked = window[offsets] * slot_mask(count, cols.shape[1])[:, :, None, None]
    return jnp.einsum("aspq,asqn->apn", blocks, picked, precision=lax.Precision.HIGHEST)


def return_rims(buffer, own_rows):
    rims = jnp.concatenate([buffer[:HB], buffer[HB + own_rows :]], axis=0)
    arrived = with_halo(rims, (("rows", 0),), HB)
    from_below = arrived[:HB]
    from_above = arrived[3 * HB :]
    owned = buffer[HB : HB + own_rows]
    owned = owned.at[:HB].add(from_below)
    owned = owned.at[own_rows - HB :].add(from_above)
    return owned


def owner_fold(values):
    return lax.psum_scatter(values, "cols", scatter_dimension=1, tiled=True)


def local(z_blocks, z_cols, z_count, h_blocks, h_cols, h_count, panel):
    own_rows = panel.shape[0]
    share_width = panel.shape[2] // lax.axis_size("cols")
    panel_share = lax.dynamic_slice_in_dim(
        panel, lax.axis_index("cols") * share_width, share_width, 2
    )
    mid_part = contract(z_blocks, z_cols, z_count, share_window(panel_share), own_rows)
    mid_share = lax.psum_scatter(mid_part, "cols", scatter_dimension=2, tiled=True)
    side_part = contract(h_blocks, h_cols, h_count, share_window(mid_share), own_rows)
    side = lax.psum(side_part, "cols")
    mask = slot_mask(z_count, z_cols.shape[1])
    terms = jnp.einsum("asqp,aqn->aspn", z_blocks, side, precision=lax.Precision.HIGHEST)
    offsets = z_cols - window_start(own_rows)
    spread = own_rows + 2 * HB
    placing = (offsets[:, :, None] == jnp.arange(spread)[None, None, :]).astype(jnp.float32)
    placing = placing * mask[:, :, None]
    buffer = jnp.einsum("asw,aspn->wpn", placing, terms, precision=lax.Precision.HIGHEST)
    owned = return_rims(buffer, own_rows)
    result = owner_fold(owned)
    return result


def solution(mesh):
    return jax.shard_map(
        local,
        mesh=mesh,
        in_specs=(
            P("rows", "cols", None, None),
            P("rows", "cols"),
            P("rows"),
            P("rows", "cols", None, None),
            P("rows", "cols"),
            P("rows"),
            P("rows", None, None),
        ),
        out_specs=P("rows", "cols", None),
        check_vma=False,
    )
```

profile of v0, /device:TPU:0, one launch (start us, length us, event | category | flops | bytes accessed | tf_op | source)
XLA Modules:
  0.0 170.3 jit_solution(8299884779458870425)
XLA Ops:
  6.5 0.9 constant_dynamic-slice_fusion
  7.5 1.3 collective-permute-start.1
  8.8 5.5 %collective-permute-start = (f32[4,256,16]{1,2,0:T(8,128)S(1)}, f32[4,256,16]{1,2,0:T(8,128)S(1)}, u32[]{:S(2)}, u32[]{:S(2)}) collective-permute-start(f32[4,256,16]{1,2,0:T(8,128)S(1)} %constant_dynamic-slice_fusion), channel_id=1, source_target_pairs={{0,4},{4,8},{8,12},{12,16},{16,20},{20,24},{24,28},{1,5},{5,9},{9,... | collective-permute-start | bytes 196616 | tf_op jit(solution)/shard_map/ppermute | solution.py:14
  14.3 0.7 compare_convert_fusion.1
  14.9 0.7 subtract_bitcast_fusion
  15.6 0.7 collective-permute-done
  16.3 8.9 %all_gather.6 = f32[12,256,64]{1,2,0:T(8,128)S(1)} all-gather(f32[12,256,16]{1,2,0:T(8,128)S(1)} %pad_maximum_fusion), channel_id=1, replica_groups=mesh['rows'=8,'cols'=4] {'cols'}, dimensions={2}, use_global_device_ids=true | all-gather | bytes 983040 | tf_op jit(solution)/shard_map/all_gather | solution.py:33
  25.3 0.6 gather_fusion
  25.8 1.8 %convolution_bitcast_fusion.1 = f32[4,256,64]{1,2,0:T(8,128)} fusion(f32[4,1,256,256]{3,2,1,0:T(8,128)S(1)} %copy-done, f32[4,256,64]{1,2,0:T(8,128)S(1)} %gather_fusion, f32[4]{0:T(128)S(1)} %compare_convert_fusion.1), kind=kOutput, calls=%fused_computation.3 | convolution fusion | flops 201392128 | bytes 1572880 | tf_op jit(solution)/shard_map/aspq,asqn->apn/dot_general | solution.py:39
  27.8 0.7 compare_convert_fusion
  28.4 0.7 fusion.18
  29.1 20.8 %reduce-scatter.5.cloned.1.call-done = f32[4,256,16]{1,2,0:T(8,128)} async-done(((f32[4,256,64]{1,2,0:T(8,128)}), f32[4,256,16]{1,2,0:T(8,128)}) %reduce-scatter.5.cloned.1.call-update) | async-done | bytes 65552 | tf_op jit(solution)/shard_map/reduce_scatter | solution.py:64
  49.9 1.3 collective-permute-start.3
  51.2 4.5 %collective-permute-start.2 = (f32[4,256,16]{1,2,0:T(8,128)}, f32[4,256,16]{1,2,0:T(8,128)S(1)}, u32[]{:S(2)}, u32[]{:S(2)}) collective-permute-start(f32[4,256,16]{1,2,0:T(8,128)} %reduce-scatter.5.cloned.1.call-done), channel_id=1, source_target_pairs={{0,4},{4,8},{8,12},{12,16},{16,20},{20,24},{24,28},{1,5},{5,9},{9,... | collective-permute-start | bytes 196616 | tf_op jit(solution)/shard_map/ppermute | solution.py:14
  55.8 0.5 collective-permute-done.3
  56.3 1.7 collective-permute-done.2
  58.0 0.9 pad_maximum_fusion.1
  58.8 7.5 %all_gather.7 = f32[12,256,64]{1,2,0:T(8,128)S(1)} all-gather(f32[12,256,16]{1,2,0:T(8,128)S(1)} %pad_maximum_fusion.1), channel_id=1, replica_groups=mesh['rows'=8,'cols'=4] {'cols'}, dimensions={2}, use_global_device_ids=true | all-gather | bytes 983040 | tf_op jit(solution)/shard_map/all_gather | solution.py:33
  66.3 0.6 gather_fusion.1
  66.9 3.1 %convolution_bitcast_fusion = f32[4,256,64]{1,2,0:T(8,128)} fusion(f32[4,1,256,256]{3,2,1,0:T(8,128)} %param.18, f32[4,256,64]{1,2,0:T(8,128)S(1)} %gather_fusion.1, f32[4]{0:T(128)S(1)} %compare_convert_fusion), kind=kOutput, calls=%fused_computation.2 | convolution fusion | flops 201392128 | bytes 1572880 | tf_op jit(solution)/shard_map/aspq,asqn->apn/dot_general | solution.py:39
  70.0 34.8 %all-reduce.2.cloned.1.call-done = f32[4,256,64]{1,2,0:T(8,128)} async-done(((f32[4,256,64]{1,2,0:T(8,128)}), f32[4,256,64]{1,2,0:T(8,128)}) %all-reduce.2.cloned.1.call-update) | async-done | bytes 262160 | tf_op jit(solution)/shard_map/psum | solution.py:66
  104.9 1.7 %fusion.1 = f32[4,64,256]{2,1,0:T(8,128)S(1)} fusion(f32[4,256,64]{1,2,0:T(8,128)} %all-reduce.2.cloned.1.call-done, f32[4,1,256,256]{3,2,1,0:T(8,128)S(1)} %copy-done), kind=kOutput, calls=%fused_computation.5 | convolution fusion | flops 201326592 | bytes 1572864 | tf_op jit(solution)/shard_map/asqp,aqn->aspn/dot_general | solution.py:68
  106.6 1.2 fusion.5
  107.9 3.4 %collective-permute-start.4 = (f32[4,256,64]{1,0,2:T(4,128)S(1)}, f32[4,256,64]{1,0,2:T(4,128)S(1)}, u32[]{:S(2)}, u32[]{:S(2)}) collective-permute-start(f32[4,256,64]{1,0,2:T(4,128)S(1)} %get-tuple-element.45), channel_id=1, source_target_pairs={{0,4},{4,8},{8,12},{12,16},{16,20},{20,24},{24,28},{1,5},{5,9},{9,... | collective-permute-start | bytes 786440 | tf_op jit(solution)/shard_map/ppermute | solution.py:14
  111.3 1.3 collective-permute-start.5
  112.6 8.7 %collective-permute-done.4 = f32[4,256,64]{1,0,2:T(4,128)S(1)} collective-permute-done((f32[4,256,64]{1,0,2:T(4,128)S(1)}, f32[4,256,64]{1,0,2:T(4,128)S(1)}, u32[]{:S(2)}, u32[]{:S(2)}) %collective-permute-start.4) | collective-permute-done | bytes 262176 | tf_op jit(solution)/shard_map/ppermute | solution.py:14
  121.3 0.1 fusion.4
  121.5 7.6 %copy.11 = f32[4,256,64]{0,2,1:T(8,128)} copy(f32[4,256,64]{1,0,2:T(4,128)S(1)} %fusion.4) | data formatting | bytes 524288
  129.0 8.9 %reshape.162 = f32[256,256]{1,0:T(8,128)} reshape(f32[256,64,4]{2,1,0:T(8,128)} %bitcast.28) | data formatting | bytes 524288
  138.0 21.5 %reduce-scatter.7.cloned.1.call-done = f32[64,256]{1,0:T(8,128)} async-done(((f32[256,256]{1,0:T(8,128)}), f32[64,256]{1,0:T(8,128)}) %reduce-scatter.7.cloned.1.call-update) | async-done | bytes 65552
  159.4 3.0 %reshape.163 = f32[64,64,4]{2,1,0:T(8,128)S(1)} reshape(f32[64,256]{1,0:T(8,128)} %reduce-scatter.7.cloned.1.call-done) | data formatting | bytes 131072
  162.4 1.4 copy.9
  (14 shorter events, 0.2 us)
Async XLA Ops:
  6.5 19.3 %copy-start = (f32[4,1,256,256]{3,2,1,0:T(8,128)S(1)}, f32[4,1,256,256]{3,2,1,0:T(8,128)}, u32[]{:S(2)}) copy-start(f32[4,1,256,256]{3,2,1,0:T(8,128)} %param.15) | copy-start | bytes 3145732
  6.5 43.4 %reduce-scatter.5.cloned.1.call-start = ((), (), s32[]{:S(2)}) async-start(), calls=%async_computation.2 | async-start | bytes 327680 | tf_op jit(solution)/shard_map/reduce_scatter | solution.py:64
  7.5 8.1 %collective-permute-start.1 = (f32[4,256,16]{1,2,0:T(8,128)S(1)}, f32[4,256,16]{1,2,0:T(8,128)S(1)}, u32[]{:S(2)}, u32[]{:S(2)}) collective-permute-start(f32[4,256,16]{1,2,0:T(8,128)S(1)} %constant_dynamic-slice_fusion), channel_id=1, source_target_pairs={{4,0},{8,4},{12,8},{16,12},{20,16},{24,20},{28,24},{5,1},{9,5},{13... | collective-permute-start | bytes 196616 | tf_op jit(solution)/shard_map/ppermute | solution.py:17
  8.8 7.5 %collective-permute-start = (f32[4,256,16]{1,2,0:T(8,128)S(1)}, f32[4,256,16]{1,2,0:T(8,128)S(1)}, u32[]{:S(2)}, u32[]{:S(2)}) collective-permute-start(f32[4,256,16]{1,2,0:T(8,128)S(1)} %constant_dynamic-slice_fusion), channel_id=1, source_target_pairs={{0,4},{4,8},{8,12},{12,16},{16,20},{20,24},{24,28},{1,5},{5,9},{9,... | collective-permute-start | bytes 196616 | tf_op jit(solution)/shard_map/ppermute | solution.py:14
  27.7 77.2 %all-reduce.2.cloned.1.call-start = ((), (), s32[]{:S(2)}) async-start(), calls=%async_computation.3 | async-start | bytes 524288 | tf_op jit(solution)/shard_map/psum | solution.py:66
  49.9 6.4 %collective-permute-start.3 = (f32[4,256,16]{1,2,0:T(8,128)}, f32[4,256,16]{1,2,0:T(8,128)S(1)}, u32[]{:S(2)}, u32[]{:S(2)}) collective-permute-start(f32[4,256,16]{1,2,0:T(8,128)} %reduce-scatter.5.cloned.1.call-done), channel_id=1, source_target_pairs={{4,0},{8,4},{12,8},{16,12},{20,16},{24,20},{28,24},{5,1},{9,5},{13... | collective-permute-start | bytes 196616 | tf_op jit(solution)/shard_map/ppermute | solution.py:17
  51.2 6.8 %collective-permute-start.2 = (f32[4,256,16]{1,2,0:T(8,128)}, f32[4,256,16]{1,2,0:T(8,128)S(1)}, u32[]{:S(2)}, u32[]{:S(2)}) collective-permute-start(f32[4,256,16]{1,2,0:T(8,128)} %reduce-scatter.5.cloned.1.call-done), channel_id=1, source_target_pairs={{0,4},{4,8},{8,12},{12,16},{16,20},{20,24},{24,28},{1,5},{5,9},{9,... | collective-permute-start | bytes 196616 | tf_op jit(solution)/shard_map/ppermute | solution.py:14
  70.0 89.5 %reduce-scatter.7.cloned.1.call-start = ((), (), s32[]{:S(2)}) async-start(), calls=%async_computation.4 | async-start | bytes 327680
  107.9 13.4 %collective-permute-start.4 = (f32[4,256,64]{1,0,2:T(4,128)S(1)}, f32[4,256,64]{1,0,2:T(4,128)S(1)}, u32[]{:S(2)}, u32[]{:S(2)}) collective-permute-start(f32[4,256,64]{1,0,2:T(4,128)S(1)} %get-tuple-element.45), channel_id=1, source_target_pairs={{0,4},{4,8},{8,12},{12,16},{16,20},{20,24},{24,28},{1,5},{5,9},{9,... | collective-permute-start | bytes 786440 | tf_op jit(solution)/shard_map/ppermute | solution.py:14
  111.3 10.0 %collective-permute-start.5 = (f32[4,256,64]{1,0,2:T(4,128)S(1)}, f32[4,256,64]{1,0,2:T(4,128)S(1)}, u32[]{:S(2)}, u32[]{:S(2)}) collective-permute-start(f32[4,256,64]{1,0,2:T(4,128)S(1)} %get-tuple-element.46), channel_id=1, source_target_pairs={{4,0},{8,4},{12,8},{16,12},{20,16},{24,20},{28,24},{5,1},{9,5},{13... | collective-permute-start | bytes 786440 | tf_op jit(solution)/shard_map/ppermute | solution.py:17
Sparse Core Ops, SparseCore 0:
  27.8 22.0 reduce-scatter.4
  70.1 34.7 all-reduce.1
  138.1 21.3 reduce-scatter.6
where the time goes:
time: 171 us; the launch traced here: 170 us
  waiting for transfers between devices  88.8 us (52%)
  local copies, waits for them, and re-layouts  23 us (13%)
  starting transfers between devices  17.4 us (10%)
  blocking collectives  16.4 us (10%)
  between operations  13.2 us (8%)
  matrix products  7.84 us (5%)
  other arithmetic  3.65 us (2%)
    psum x1, waiting for transfers between devices, local(): side = lax.psum(side_part, 'cols')  34.8 us
    unnamed x4, waiting for transfers between devices  21.5 us
    reduce_scatter x1, waiting for transfers between devices, local(): lax.psum_scatter(mid_part, 'cols', scatter_dimension=2, tiled=True)  20.8 us
    unnamed x5, local copies, waits for them, and re-layouts  19.5 us
    all_gather x2, blocking collectives, share_window(): return lax.all_gather(arrived, 'cols', axis=2, tiled=True)  16.4 us
    ppermute x3, starting transfers between devices, with_halo(): lax.ppermute(lax.slice_in_dim(block, block.shape[dim] - width, None, axis...  13.4 us
    ppermute x3, waiting for transfers between devices, with_halo(): lax.ppermute(lax.slice_in_dim(block, block.shape[dim] - width, None, axis...  11.1 us
    dot_general x2, matrix products, contract(): jnp.einsum('aspq,asqn->apn', blocks, picked, precision=lax.Precision.HIGH...  4.9 us
  transfers between devices with their start and end apart: 9, of which 7 were waited for; matrix products, arithmetic and copies ran while one was open for 2% of the time, Pallas kernels for 0%

commit v1 on v0

v1 whole, which is shorter than its diff:
```python
import functools

import jax
import jax.numpy as jnp
from jax import lax
from jax.experimental import pallas as pl
from jax.experimental.pallas import tpu as pltpu
from jax.sharding import PartitionSpec as P

MESH = pl.DeviceIdType.MESH
BF = jnp.bfloat16
F32 = jnp.float32


def split(x):
    hi = x.astype(BF)
    return hi, (x - hi.astype(F32)).astype(BF)


def kernel(nr, nc, own, blk, width,
           zc, zn, hc, hn, z_hbm, h_hbm, p_hbm, out,
           pan, zf, hf, zhi, zlo, thi, tlo, hhi, hlo,
           codes, codes_all, idx,
           xwin, xsend, xpick, mpart, mrecv, mwin, msend, mpick,
           spart, srecv, side, term, trecv, acc, below, above,
           local_sem, idx_sem, peer_send, peer_recv, row_send, row_recv):
    r, c = lax.axis_index("rows"), lax.axis_index("cols")
    sh = blk // nc
    np_ = own // 2
    lanes = 2 * width
    has_low, has_high = r > 0, r < nr - 1
    mine = pl.ds(pl.multiple_of(c * sh, sh), sh)

    def peer(d):
        return lax.rem(c + d, nc)

    def rows_of(q):
        return pl.ds(pl.multiple_of(q * sh, sh), sh)

    load_p = pltpu.make_async_copy(p_hbm.at[:, mine, :], pan, local_sem.at[0])
    load_z = pltpu.make_async_copy(z_hbm.at[:, 0], zf, local_sem.at[1])
    load_h = pltpu.make_async_copy(h_hbm.at[:, 0], hf, local_sem.at[2])
    load_p.start()
    load_z.start()
    load_h.start()

    barrier = pltpu.get_barrier_semaphore()
    for d in range(1, nc):
        pl.semaphore_signal(barrier, inc=1, device_id=(r, peer(d)), device_id_type=MESH)

    @pl.when(has_low)
    def _():
        pl.semaphore_signal(barrier, inc=1, device_id=(r - 1, c), device_id_type=MESH)

    @pl.when(has_high)
    def _():
        pl.semaphore_signal(barrier, inc=1, device_id=(r + 1, c), device_id_type=MESH)

    lane = lax.broadcasted_iota(jnp.int32, (1, lanes), 1)
    left = lane < width
    code_row = lax.broadcasted_iota(jnp.int32, (8, 128), 0)
    start = r * own - own
    code = jnp.zeros((8, 128), jnp.int32) - 1
    for a in range(own):
        zo = jnp.where(c < zn[a], zc[a, 0] - start, -1)
        ho = jnp.where(c < hn[a], hc[a, 0] - start, -1)
        code = jnp.where(code_row == a, zo, code)
        code = jnp.where(code_row == own + a, ho, code)
    codes[...] = code

    load_p.wait()
    for j in range(np_):
        xwin[np_ + j] = jnp.concatenate([pan[2 * j], pan[2 * j + 1]], axis=1)

    pl.semaphore_wait(barrier, nc - 1 + has_low.astype(jnp.int32) + has_high.astype(jnp.int32))

    def exchange(k, low_src, high_src, low_dst, high_dst):
        down = pltpu.make_async_remote_copy(
            low_src, high_dst, row_send.at[k, 0], row_recv.at[k, 0],
            device_id=(r - 1, c), device_id_type=MESH)
        up = pltpu.make_async_remote_copy(
            high_src, low_dst, row_send.at[k, 1], row_recv.at[k, 1],
            device_id=(r + 1, c), device_id_type=MESH)

        @pl.when(has_low)
        def _():
            down.start()

        @pl.when(has_high)
        def _():
            up.start()

        def arrive():
            @pl.when(has_low)
            def _():
                up.wait_recv()
                down.wait_send()

            @pl.when(has_high)
            def _():
                down.wait_recv()
                up.wait_send()
        return arrive

    def to_peers(k, src_of, dst_of):
        copies = []
        for d in range(1, nc):
            copies.append(pltpu.make_async_remote_copy(
                src_of(d), dst_of(d), peer_send.at[k, d - 1], peer_recv.at[k, d - 1],
                device_id=(r, peer(d)), device_id_type=MESH))
            copies[-1].start()

        def arrive():
            for copy in copies:
                copy.wait_recv()

        def sent():
            for copy in copies:
                copy.wait_send()
        return arrive, sent

    got0 = exchange(0, xwin.at[pl.ds(np_, np_)], xwin.at[pl.ds(np_, np_)],
                    xwin.at[pl.ds(0, np_)], xwin.at[pl.ds(2 * np_, np_)])
    got_codes, sent_codes = to_peers(0, lambda d: codes, lambda d: codes_all.at[d])
    codes_all[0] = code

    for win in (xwin, mwin):
        @pl.when(r == 0)
        def _():
            win[pl.ds(0, np_)] = jnp.zeros((np_, sh, lanes), F32)

        @pl.when(r == nr - 1)
        def _():
            win[pl.ds(2 * np_, np_)] = jnp.zeros((np_, sh, lanes), F32)

    load_z.wait()
    for a in range(own):
        z = zf[a]
        zhi[a], zlo[a] = split(z)
    got_codes()
    to_smem = pltpu.make_async_copy(codes_all, idx, idx_sem)
    to_smem.start()
    to_smem.wait()

    def code_of(d, row):
        return idx[(nc - d) % nc, row, 0]

    def pick(win, d, base, send, own_dst):
        for j in range(np_):
            halves = []
            for h in range(2):
                off = code_of(d, base + 2 * j + h)
                at = jnp.maximum(off, 0)
                pair = win[at // 2]
                swapped = pltpu.roll(pair, width, 1)
                use = jnp.where(at % 2 == h, pair, swapped)
                halves.append(jnp.where(off >= 0, use, 0.0))
            both = jnp.where(left, halves[0], halves[1])
            if d == 0:
                own_dst[j, mine, :] = both
            else:
                send[d - 1, j] = both

    def apply(hi_ref, lo_ref, src, dst):
        for j in range(np_):
            hi, lo = split(src[j])
            cat = jnp.concatenate([hi, lo], axis=1)
            res = []
            for a in (2 * j, 2 * j + 1):
                wide = jnp.dot(hi_ref[a], cat, preferred_element_type=F32)
                slim = jnp.dot(lo_ref[a], hi, preferred_element_type=F32)
                res.append(wide[:, :lanes] + (wide[:, lanes:] + slim))
            dst[j] = jnp.where(left, res[0], res[1])

    def pick_all(k, win, base, send, dst):
        copies = []
        for d in list(range(1, nc)) + [0]:
            pick(win, d, base, send, dst)
            if d:
                copies.append(pltpu.make_async_remote_copy(
                    send.at[d - 1], dst.at[:, mine, :],
                    peer_send.at[k, d - 1], peer_recv.at[k, d - 1],
                    device_id=(r, peer(d)), device_id_type=MESH))
                copies[-1].start()
        return copies

    def recv_all(copies, dst, k):
        for d in range(1, nc):
            q = lax.rem(c + nc - d, nc)
            pltpu.make_async_remote_copy(
                dst.at[:, rows_of(q), :], dst.at[:, rows_of(q), :],
                peer_send.at[k, d - 1], peer_recv.at[k, d - 1],
                device_id=(r, peer(d)), device_id_type=MESH).wait_recv()

    got0()
    copies_x = pick_all(1, xwin, 0, xsend, xpick)
    load_h.wait()
    for a in range(own):
        hhi[a], hlo[a] = split(hf[a])
    recv_all(copies_x, xpick, 1)
    apply(zhi, zlo, xpick, mpart)

    def reduce(k, part, recv, store):
        arrive, sent = to_peers(k, lambda d: part.at[:, rows_of(peer(d)), :],
                                lambda d: recv.at[d - 1])
        if k == 2:
            for a in range(own):
                thi[a], tlo[a] = split(zf[a].T)
        arrive()
        for j in range(np_):
            total = part[j, mine, :]
            for d in range(1, nc):
                total = total + recv[d - 1, j]
            store(j, total)
        return sent

    def store_mid(j, v):
        mwin[np_ + j] = v

    sent_m = reduce(2, mpart, mrecv, store_mid)
    got1 = exchange(1, mwin.at[pl.ds(np_, np_)], mwin.at[pl.ds(np_, np_)],
                    mwin.at[pl.ds(0, np_)], mwin.at[pl.ds(2 * np_, np_)])
    got1()
    copies_m = pick_all(3, mwin, own, msend, mpick)
    recv_all(copies_m, mpick, 3)
    apply(hhi, hlo, mpick, spart)

    def store_side(j, v):
        side[j, mine, :] = v

    sent_s = reduce(4, spart, srecv, store_side)
    copies_s = []
    for d in range(1, nc):
        copies_s.append(pltpu.make_async_remote_copy(
            side.at[:, mine, :], side.at[:, mine, :],
            peer_send.at[5, d - 1], peer_recv.at[5, d - 1],
            device_id=(r, peer(d)), device_id_type=MESH))
        copies_s[-1].start()
    recv_all(copies_s, side, 5)
    apply(thi, tlo, side, term)

    arrive_t, sent_t = to_peers(6, lambda d: term.at[:, rows_of(peer(d)), :],
                                lambda d: trecv.at[d - 1])
    sums = [jnp.zeros((sh, lanes), F32) for _ in range(3 * np_)]
    half = jnp.where(left, 0, 1)
    for d in range(nc):
        if d == 1:
            arrive_t()
        for j in range(np_):
            t = term[j, mine, :] if d == 0 else trecv[d - 1, j]
            swapped = pltpu.roll(t, width, 1)
            for h in range(2):
                dup = jnp.where(left, t, swapped) if h == 0 else jnp.where(left, swapped, t)
                off = idx[d, 2 * j + h, 0]
                for p in range(3 * np_):
                    sums[p] = sums[p] + jnp.where(half == off - 2 * p, dup, 0.0)
    for p in range(3 * np_):
        acc[p] = sums[p]
    got2 = exchange(2, acc.at[pl.ds(0, np_)], acc.at[pl.ds(2 * np_, np_)], below, above)

    @pl.when(r == 0)
    def _():
        below[...] = jnp.zeros(below.shape, F32)

    @pl.when(r == nr - 1)
    def _():
        above[...] = jnp.zeros(above.shape, F32)

    sent_codes()
    for copy in copies_x + copies_m + copies_s:
        copy.wait_send()
    sent_m()
    sent_s()
    sent_t()
    got2()
    for j in range(np_):
        total = acc[np_ + j] + below[j] + above[j]
        out[2 * j] = total[:, :width]
        out[2 * j + 1] = total[:, width:]


def local(nr, nc, z_blocks, z_cols, z_count, h_blocks, h_cols, h_count, panel):
    own, blk, width = panel.shape
    sh, np_, lanes = blk // nc, own // 2, 2 * width
    f = lambda *s: pltpu.VMEM(s, F32)
    b = lambda *s: pltpu.VMEM(s, BF)
    dma = pltpu.SemaphoreType.DMA
    smem = pl.BlockSpec(memory_space=pltpu.SMEM)
    hbm = pl.BlockSpec(memory_space=pl.ANY)
    full = (np_, blk, lanes)
    peers = (nc - 1, np_, sh, lanes)
    return pl.pallas_call(
        functools.partial(kernel, nr, nc, own, blk, width),
        out_shape=jax.ShapeDtypeStruct((own, sh, width), F32),
        in_specs=[smem] * 4 + [hbm] * 3,
        out_specs=pl.BlockSpec(memory_space=pltpu.VMEM),
        scratch_shapes=[
            f(own, sh, width), f(own, blk, blk), f(own, blk, blk),
            b(own, blk, blk), b(own, blk, blk), b(own, blk, blk),
            b(own, blk, blk), b(own, blk, blk), b(own, blk, blk),
            pltpu.VMEM((8, 128), jnp.int32), pltpu.VMEM((nc, 8, 128), jnp.int32),
            pltpu.SMEM((nc, 8, 128), jnp.int32),
            f(3 * np_, sh, lanes), f(*peers), f(*full), f(*full), f(*peers),
            f(3 * np_, sh, lanes), f(*peers), f(*full),
            f(*full), f(*peers), f(*full), f(*full), f(*peers),
            f(3 * np_, sh, lanes), f(np_, sh, lanes), f(np_, sh, lanes),
            dma((3,)), dma, dma((7, nc - 1)), dma((7, nc - 1)), dma((3, 2)), dma((3, 2)),
        ],
        compiler_params=pltpu.CompilerParams(
            collective_id=0, has_side_effects=True, vmem_limit_bytes=32 * 1024 * 1024),
    )(z_cols, z_count, h_cols, h_count, z_blocks, h_blocks, panel)


def solution(mesh):
    return jax.shard_map(
        functools.partial(local, mesh.shape["rows"], mesh.shape["cols"]),
        mesh=mesh,
        in_specs=(
            P("rows", "cols", None, None),
            P("rows", "cols"),
            P("rows"),
            P("rows", "cols", None, None),
            P("rows", "cols"),
            P("rows"),
            P("rows", None, None),
        ),
        out_specs=P("rows", "cols", None),
        check_vma=False,
    )
```

time: 171 us -> 50 us (0.29)
  the two profiles are of different devices: /device:TPU:0 before, /device:TPU:17 now
where the time goes in v1:
time: 50 us; the launch traced here: 49.8 us
  Pallas kernels  44.6 us (89%)
  local copies, waits for them, and re-layouts  5.13 us (10%)
    pallas_call x1, Pallas kernels, local(): pl.pallas_call(functools.partial(kernel, nr, nc, own, blk, width), out_sh...  44.6 us
    unnamed x14, local copies, waits for them, and re-layouts  5.13 us

profile of v1, /device:TPU:17, one launch (start us, length us, event | category | flops | bytes accessed | tf_op | source)
XLA Modules:
  0.0 49.8 jit_solution(10896645639495935707)
XLA Ops:
  0.0 0.0 copy-start.4
  0.0 0.8 %copy.8.zc = s32[4,1]{1,0:T(4,128)S(1)} copy(s32[4,1]{0,1:T(1,128)} %param.8) | data formatting | bytes 32 | tf_op args[1]
  0.8 0.0 copy-done.4
  0.8 0.1 copy.9.hc
  0.9 0.0 copy-start.2
  0.9 0.0 copy-start.3
  0.9 1.2 %copy.10.p_hbm = f32[4,256,64]{2,1,0:T(8,128)S(1)} copy(f32[4,256,64]{1,2,0:T(8,128)} %param.13) | data formatting | bytes 524288 | tf_op args[6]
  2.0 0.0 copy-done.2
  2.0 0.0 copy-done.3
  2.1 0.0 copy-start
  2.1 1.2 %copy-done = f32[4,1,256,256]{3,2,1,0:T(8,128)S(1)} copy-done((f32[4,1,256,256]{3,2,1,0:T(8,128)S(1)}, f32[4,1,256,256]{3,2,1,0:T(8,128)}, u32[]{:S(2)}) %copy-start) | copy-done | bytes 1048600
  3.3 0.0 copy-start.1
  3.3 1.2 %copy-done.1 = f32[4,1,256,256]{3,2,1,0:T(8,128)S(1)} copy-done((f32[4,1,256,256]{3,2,1,0:T(8,128)S(1)}, f32[4,1,256,256]{3,2,1,0:T(8,128)}, u32[]{:S(2)}) %copy-start.1) | copy-done | bytes 1048600
  4.5 44.6 %shard_map.73 = f32[4,64,64]{2,1,0:T(8,128)S(1)} custom-call(s32[4,1]{1,0:T(4,128)S(1)} %copy.8.zc, s32[4]{0:T(128)S(1)} %copy-done.2, s32[4,1]{1,0:T(4,128)S(1)} %copy.9.hc, s32[4]{0:T(128)S(1)} %copy-done.3, f32[4,1,256,256]{3,2,1,0:T(8,128)S(1)} %copy-done, f32[4,1,256,256]{3,2,1,0:T(8,128)S(1)} %copy-done.1, f32[4,256,64]{2,1,0:T(8,128)S(1)} %copy.10.p_hbm), custom_call_target="tpu_custom_call" | custom-call | tf_op jit(solution)/shard_map/pallas_call | solution.py:292
  49.1 0.7 %copy.12 = f32[4,64,64]{2,1,0:T(8,128)} copy(f32[4,64,64]{2,1,0:T(8,128)S(1)} %shard_map.73) | data formatting | bytes 131072
Async XLA Ops:
  0.0 0.8 %copy-start.4 = (s32[4,1]{0,1:T(1,128)S(1)}, s32[4,1]{0,1:T(1,128)}, u32[]{:S(2)}) copy-start(s32[4,1]{0,1:T(1,128)} %param.11) | copy-start | bytes 52
  0.9 1.2 %copy-start.2 = (s32[4]{0:T(128)S(1)}, s32[4]{0:T(128)}, u32[]{:S(2)}) copy-start(s32[4]{0:T(128)} %zn.1) | copy-start | bytes 52
  0.9 1.2 %copy-start.3 = (s32[4]{0:T(128)S(1)}, s32[4]{0:T(128)}, u32[]{:S(2)}) copy-start(s32[4]{0:T(128)} %hn.1) | copy-start | bytes 52
  2.1 1.2 %copy-start = (f32[4,1,256,256]{3,2,1,0:T(8,128)S(1)}, f32[4,1,256,256]{3,2,1,0:T(8,128)}, u32[]{:S(2)}) copy-start(f32[4,1,256,256]{3,2,1,0:T(8,128)} %z_hbm.1) | copy-start | bytes 3145732
  3.3 1.2 %copy-start.1 = (f32[4,1,256,256]{3,2,1,0:T(8,128)S(1)}, f32[4,1,256,256]{3,2,1,0:T(8,128)}, u32[]{:S(2)}) copy-start(f32[4,1,256,256]{3,2,1,0:T(8,128)} %h_hbm.1) | copy-start | bytes 3145732

commit v2 on v0

v2 whole, which is shorter than its diff:
```python
import functools

import jax
import jax.numpy as jnp
from jax import lax
from jax.experimental import pallas as pl
from jax.experimental.pallas import tpu as pltpu
from jax.sharding import PartitionSpec as P

MESH = pl.DeviceIdType.MESH
BF = jnp.bfloat16
F32 = jnp.float32


def split(x):
    hi = x.astype(BF)
    return hi, (x - hi.astype(F32)).astype(BF)


def kernel(nr, nc, own, blk, width, w,
           zc, zn, hc, hn, z_hbm, h_hbm, p_hbm, out,
           pan, zf, hf, zhi, zlo, thi, tlo, hhi, hlo,
           codes, codes_all, idx, xfull, xwin, xsend, xpick, mpart, mrecv, mwin, msend, mpick,
           spart, srecv, side, term, trecv, acc, rims,
           local_sem, idx_sem, code_send, code_recv,
           peer_send, peer_recv, row_send, row_recv):
    r, c = lax.axis_index("rows"), lax.axis_index("cols")
    sh = blk // nc
    lanes = own * w
    has_low, has_high = r > 0, r < nr - 1

    def peer(d):
        return lax.rem(c + d, nc)

    def rows_of(q):
        return pl.ds(pl.multiple_of(q * sh, sh), sh)

    mine = rows_of(c)
    load_p = pltpu.make_async_copy(p_hbm, pan, local_sem.at[0])
    load_z = pltpu.make_async_copy(z_hbm.at[:, 0], zf, local_sem.at[1])
    load_h = pltpu.make_async_copy(h_hbm.at[:, 0], hf, local_sem.at[2])
    load_p.start()
    load_z.start()
    load_h.start()

    barrier = pltpu.get_barrier_semaphore()
    for d in range(1, nc):
        pl.semaphore_signal(barrier, inc=1, device_id=(r, peer(d)), device_id_type=MESH)

    @pl.when(has_low)
    def _():
        pl.semaphore_signal(barrier, inc=1, device_id=(r - 1, c), device_id_type=MESH)

    @pl.when(has_high)
    def _():
        pl.semaphore_signal(barrier, inc=1, device_id=(r + 1, c), device_id_type=MESH)

    part_of_lane = lax.broadcasted_iota(jnp.int32, (1, lanes), 1) // w
    code_row = lax.broadcasted_iota(jnp.int32, (8, 128), 0)
    start = r * own - own
    code = jnp.zeros((8, 128), jnp.int32) - 1
    for a in range(own):
        zo = jnp.where(c < zn[a], zc[a] - start, -1)
        ho = jnp.where(c < hn[a], hc[a] - start, -1)
        code = jnp.where(code_row == a, zo, code)
        code = jnp.where(code_row == own + a, ho, code)
    codes[...] = code
    codes_all[0] = code

    chains = width // w
    load_p.wait()
    for g in range(chains):
        flat = jnp.concatenate([pan[a, g * w:(g + 1) * w, :] for a in range(own)], axis=0)
        xfull[g] = flat.T
        xwin[g, 1] = xfull[g, mine, :]

    for win in (xwin, mwin):
        @pl.when(r == 0)
        def _():
            win[:, 0] = jnp.zeros((chains, sh, lanes), F32)

        @pl.when(r == nr - 1)
        def _():
            win[:, 2] = jnp.zeros((chains, sh, lanes), F32)

    @pl.when(r == 0)
    def _():
        rims[:, 0] = jnp.zeros((chains, sh, lanes), F32)

    @pl.when(r == nr - 1)
    def _():
        rims[:, 1] = jnp.zeros((chains, sh, lanes), F32)

    pl.semaphore_wait(barrier, nc - 1 + has_low.astype(jnp.int32) + has_high.astype(jnp.int32))

    unsent = []

    def exchange(g, k, to_low, to_high, from_low, from_high):
        down = pltpu.make_async_remote_copy(
            to_low, from_high, row_send.at[g, k, 0], row_recv.at[g, k, 0],
            device_id=(r - 1, c), device_id_type=MESH)
        up = pltpu.make_async_remote_copy(
            to_high, from_low, row_send.at[g, k, 1], row_recv.at[g, k, 1],
            device_id=(r + 1, c), device_id_type=MESH)

        @pl.when(has_low)
        def _():
            down.start()

        @pl.when(has_high)
        def _():
            up.start()

        def arrive():
            @pl.when(has_low)
            def _():
                up.wait_recv()

            @pl.when(has_high)
            def _():
                down.wait_recv()

        def sent():
            @pl.when(has_low)
            def _():
                down.wait_send()

            @pl.when(has_high)
            def _():
                up.wait_send()
        unsent.append(sent)
        return arrive

    def send(g, k, d, src, dst):
        copy = pltpu.make_async_remote_copy(
            src, dst, peer_send.at[g, k, d - 1], peer_recv.at[g, k, d - 1],
            device_id=(r, peer(d)), device_id_type=MESH)
        copy.start()
        unsent.append(copy.wait_send)
        return copy

    def arrive_rows(g, k, dst):
        for d in range(1, nc):
            here = dst.at[rows_of(lax.rem(c + nc - d, nc)), :]
            pltpu.make_async_remote_copy(
                here, here, peer_send.at[g, k, d - 1], peer_recv.at[g, k, d - 1],
                device_id=(r, peer(d)), device_id_type=MESH).wait_recv()

    def everywhere(x):
        step = lanes // 2
        while step >= w:
            x = x + pltpu.roll(x, step, 1)
            step //= 2
        return x

    def picks(g, k, win, base, buf, dst):
        for d in list(range(1, nc)) + [0]:
            both = jnp.zeros((sh, lanes), F32)
            for h in range(own):
                off = idx[(nc - d) % nc, base + h, 0]
                one = jnp.zeros((sh, lanes), F32)
                for p in range(3):
                    one = jnp.where(part_of_lane == off - own * p, win[p], one)
                both = jnp.where(part_of_lane == h, everywhere(one), both)
            if d:
                buf[d - 1] = both
                send(g, k, d, buf.at[d - 1], dst.at[mine, :])
            else:
                dst[mine, :] = both

    def apply(hi_ref, lo_ref, src, dst):
        hi, lo = split(src[...])
        cat = jnp.concatenate([hi, lo], axis=1)
        res = None
        for a in range(own):
            wide = jnp.dot(hi_ref[a], cat, preferred_element_type=F32)
            slim = jnp.dot(lo_ref[a], hi, preferred_element_type=F32)
            one = wide[:, :lanes] + (wide[:, lanes:] + slim)
            res = one if a == 0 else jnp.where(part_of_lane == a, one, res)
        dst[...] = res

    def scatter(g, k, part, recv):
        return [send(g, k, d, part.at[rows_of(peer(d)), :], recv.at[d - 1])
                for d in range(1, nc)]

    def total(part, recv, copies):
        value = part[mine, :]
        for d in range(1, nc):
            copies[d - 1].wait_recv()
            value = value + recv[d - 1]
        return value

    def chain(g):
        xw, mw = xwin.at[g], mwin.at[g]
        got = exchange(g, 0, xw.at[1], xw.at[1], xw.at[0], xw.at[2])
        yield
        got()
        picks(g, 0, xw, 0, xsend.at[g], xpick.at[g])
        yield
        arrive_rows(g, 0, xpick.at[g])
        apply(zhi, zlo, xpick.at[g], mpart.at[g])
        copies = scatter(g, 1, mpart.at[g], mrecv.at[g])
        yield
        mw[1] = total(mpart.at[g], mrecv.at[g], copies)
        got = exchange(g, 1, mw.at[1], mw.at[1], mw.at[0], mw.at[2])
        yield
        got()
        picks(g, 2, mw, own, msend.at[g], mpick.at[g])
        yield
        arrive_rows(g, 2, mpick.at[g])
        apply(hhi, hlo, mpick.at[g], spart.at[g])
        copies = scatter(g, 3, spart.at[g], srecv.at[g])
        yield
        whole = side.at[g]
        whole[mine, :] = total(spart.at[g], srecv.at[g], copies)
        for d in range(1, nc):
            send(g, 4, d, whole.at[mine, :], whole.at[mine, :])
        yield
        arrive_rows(g, 4, whole)
        apply(thi, tlo, whole, term.at[g])
        copies = scatter(g, 5, term.at[g], trecv.at[g])
        yield
        sums = [jnp.zeros((sh, lanes), F32) for _ in range(3)]
        for d in range(nc):
            if d:
                copies[d - 1].wait_recv()
            t = trecv[g, d - 1] if d else term[g, mine, :]
            for a in range(own):
                off = idx[d, a, 0]
                dup = everywhere(jnp.where(part_of_lane == a, t, 0.0))
                for p in range(3):
                    sums[p] = sums[p] + jnp.where(part_of_lane == off - own * p, dup, 0.0)
        for p in range(3):
            acc[g, p] = sums[p]
        got = exchange(g, 2, acc.at[g, 0], acc.at[g, 2], rims.at[g, 0], rims.at[g, 1])
        yield
        got()

    def advance():
        for one in running:
            next(one, None)

    running = [chain(g) for g in range(chains)]
    code_copies = []
    for d in range(1, nc):
        code_copies.append(pltpu.make_async_remote_copy(
            codes, codes_all.at[d], code_send.at[d - 1], code_recv.at[d - 1],
            device_id=(r, peer(d)), device_id_type=MESH))
        code_copies[-1].start()
    advance()
    load_z.wait()
    for a in range(own):
        zhi[a], zlo[a] = split(zf[a])
    for copy in code_copies:
        copy.wait_recv()
    to_smem = pltpu.make_async_copy(codes_all, idx, idx_sem)
    to_smem.start()
    to_smem.wait()
    advance()
    load_h.wait()
    for a in range(own):
        hhi[a], hlo[a] = split(hf[a])
    advance()
    for a in range(own):
        thi[a], tlo[a] = split(zf[a].T)
    for _ in range(6):
        advance()
    for copy in code_copies:
        copy.wait_send()
    for sent in unsent:
        sent()
    advance()
    sums = [acc[g, 1] + rims[g, 0] + rims[g, 1] for g in range(chains)]
    for a in range(own):
        out[a] = jnp.concatenate([s[:, a * w:(a + 1) * w] for s in sums], axis=1)


def local(nr, nc, z_blocks, z_cols, z_count, h_blocks, h_cols, h_count, panel):
    own, blk, width = panel.shape
    w = min(width, 128 // own)
    g, sh, lanes = width // w, blk // nc, own * w
    f = lambda *s: pltpu.VMEM(s, F32)
    halves = pltpu.VMEM((own, blk, blk), BF)
    dma = pltpu.SemaphoreType.DMA
    smem = pl.BlockSpec(memory_space=pltpu.SMEM)
    hbm = pl.BlockSpec(memory_space=pltpu.HBM)
    full, peers, window = f(g, blk, lanes), f(g, nc - 1, sh, lanes), f(g, 3, sh, lanes)
    return pl.pallas_call(
        functools.partial(kernel, nr, nc, own, blk, width, w),
        out_shape=jax.ShapeDtypeStruct((own, sh, width), F32),
        in_specs=[smem] * 4 + [hbm] * 3,
        out_specs=pl.BlockSpec(memory_space=pltpu.VMEM),
        scratch_shapes=[
            f(own, width, blk), f(own, blk, blk), f(own, blk, blk),
        ] + [halves] * 6 + [
            pltpu.VMEM((8, 128), jnp.int32), pltpu.VMEM((nc, 8, 128), jnp.int32),
            pltpu.SMEM((nc, 8, 128), jnp.int32),
            full, window, peers, full, full, peers, window, peers, full,
            full, peers, full, full, peers, window, f(g, 2, sh, lanes),
            dma((3,)), dma, dma((nc - 1,)), dma((nc - 1,)),
            dma((g, 6, nc - 1)), dma((g, 6, nc - 1)), dma((g, 3, 2)), dma((g, 3, 2)),
        ],
        compiler_params=pltpu.CompilerParams(
            collective_id=0, has_side_effects=True, vmem_limit_bytes=60 * 1024 * 1024),
    )(z_cols.reshape(-1), z_count, h_cols.reshape(-1), h_count, z_blocks, h_blocks,
      jnp.swapaxes(panel, 1, 2))


def solution(mesh):
    return jax.shard_map(
        functools.partial(local, mesh.shape["rows"], mesh.shape["cols"]),
        mesh=mesh,
        in_specs=(
            P("rows", "cols", None, None),
            P("rows", "cols"),
            P("rows"),
            P("rows", "cols", None, None),
            P("rows", "cols"),
            P("rows"),
            P("rows", None, None),
        ),
        out_specs=P("rows", "cols", None),
        check_vma=False,
    )
```

time: 171 us -> 42.2 us (0.25)
  waiting for transfers between devices: 88.8 us -> 0 us
  Pallas kernels: 0 us -> 40.5 us
  local copies, waits for them, and re-layouts: 23 us -> 1.57 us
  starting transfers between devices: 17.4 us -> 0 us
  blocking collectives: 16.4 us -> 0 us
  between operations: 13.2 us -> 0.01 us
  matrix products: 7.84 us -> 0 us
  other arithmetic: 3.65 us -> 0 us
    pallas_call x0 -> x1, Pallas kernels: none -> 40.5 us  [local(): pl.pallas_call(functools.partial(kernel, nr, nc, own, blk, width, w), out...]
    psum x1 -> x0, waiting for transfers between devices: 34.8 us -> none  [local(): side = lax.psum(side_part, 'cols')]
    unnamed x4 -> x0, waiting for transfers between devices: 21.5 us -> none
    reduce_scatter x1 -> x0, waiting for transfers between devices: 20.8 us -> none  [local(): lax.psum_scatter(mid_part, 'cols', scatter_dimension=2, tiled=True)]
    unnamed x5 -> x1, local copies, waits for them, and re-layouts: 19.5 us -> 1.57 us
    ppermute x6 -> x0, starting transfers between devices: 17.3 us -> none  [the longest x3 13.4 us: with_halo(): lax.ppermute(lax.slice_in_dim(block, block.shape[dim] - width, None, axis...]
    all_gather x2 -> x0, blocking collectives: 16.4 us -> none  [share_window(): return lax.all_gather(arrived, 'cols', axis=2, tiled=True)]
    ppermute x6 -> x0, waiting for transfers between devices: 11.6 us -> none  [the longest x3 11.1 us: with_halo(): lax.ppermute(lax.slice_in_dim(block, block.shape[dim] - width, None, axis...]
  transfers between devices with their start and end apart: 9 -> 0, of which waited for: 7 -> 0; matrix products, arithmetic and copies ran while one was open for 2% -> 0% of each run, Pallas kernels for 0% -> 0%
where the time goes in v2:
time: 42.2 us; the launch traced here: 42.1 us
  Pallas kernels  40.5 us (96%)
  local copies, waits for them, and re-layouts  1.57 us (4%)
    pallas_call x1, Pallas kernels, local(): pl.pallas_call(functools.partial(kernel, nr, nc, own, blk, width, w), out...  40.5 us
    unnamed x1, local copies, waits for them, and re-layouts  1.57 us

profile of v2, /device:TPU:0, one launch (start us, length us, event | category | flops | bytes accessed | tf_op | source)
XLA Modules:
  0.0 42.1 jit_solution(7565871637668171468)
XLA Ops:
  0.0 40.5 %shard_map.73 = f32[4,64,64]{2,1,0:T(8,128)} custom-call(s32[4]{0:T(128)} %bitcast.4, s32[4]{0:T(128)} %zn.1, s32[4]{0:T(128)} %bitcast.5, s32[4]{0:T(128)} %hn.1, f32[4,1,256,256]{3,2,1,0:T(8,128)} %z_hbm.1, f32[4,1,256,256]{3,2,1,0:T(8,128)} %h_hbm.1, f32[4,64,256]{2,1,0:T(8,128)} %bitcast.3), custom_call_target="tpu_custom_call" | custom-call | tf_op jit(solution)/shard_map/pallas_call | solution.py:288
  40.5 1.6 %copy.9 = f32[4,64,64]{2,1,0:T(8,128)} copy(f32[4,64,64]{2,1,0:T(8,128)} %shard_map.73) | data formatting | bytes 131072

commit v3 on v2

--- a/solution.py
+++ b/solution.py
@@ -21,12 +21,14 @@
            zc, zn, hc, hn, z_hbm, h_hbm, p_hbm, out,
            pan, zf, hf, zhi, zlo, thi, tlo, hhi, hlo,
            codes, codes_all, idx, xfull, xwin, xsend, xpick, mpart, mrecv, mwin, msend, mpick,
-           spart, srecv, side, term, trecv, acc, rims,
+           spart, srecv, side, term, trecv, acc, rims, mpair, spair, mhalf, shalf,
            local_sem, idx_sem, code_send, code_recv,
            peer_send, peer_recv, row_send, row_recv):
     r, c = lax.axis_index("rows"), lax.axis_index("cols")
     sh = blk // nc
     lanes = own * w
+    nx = nc // 2
+    x, core = c // 2, lax.rem(c, 2)
     has_low, has_high = r > 0, r < nr - 1
 
     def peer(d):
@@ -131,10 +133,10 @@
         unsent.append(sent)
         return arrive
 
-    def send(g, k, d, src, dst):
+    def send(g, k, d, src, dst, target=None):
         copy = pltpu.make_async_remote_copy(
             src, dst, peer_send.at[g, k, d - 1], peer_recv.at[g, k, d - 1],
-            device_id=(r, peer(d)), device_id_type=MESH)
+            device_id=(r, peer(d) if target is None else target), device_id_type=MESH)
         copy.start()
         unsent.append(copy.wait_send)
         return copy
@@ -169,7 +171,7 @@
                 dst[mine, :] = both
 
     def apply(hi_ref, lo_ref, src, dst):
-        hi, lo = split(src[...])
+        hi, lo = split(src[...].reshape(blk, lanes))
         cat = jnp.concatenate([hi, lo], axis=1)
         res = None
         for a in range(own):
@@ -177,18 +179,17 @@
             slim = jnp.dot(lo_ref[a], hi, preferred_element_type=F32)
             one = wide[:, :lanes] + (wide[:, lanes:] + slim)
             res = one if a == 0 else jnp.where(part_of_lane == a, one, res)
-        dst[...] = res
+        dst[...] = res.reshape(dst.shape)
 
     def scatter(g, k, part, recv):
         return [send(g, k, d, part.at[rows_of(peer(d)), :], recv.at[d - 1])
                 for d in range(1, nc)]
 
-    def total(part, recv, copies):
-        value = part[mine, :]
-        for d in range(1, nc):
-            copies[d - 1].wait_recv()
-            value = value + recv[d - 1]
-        return value
+    def to_partner(g, k, part, recv):
+        return send(g, k, 1, part.at[:, 1 - core], recv, c + 1 - 2 * core)
+
+    def across(d):
+        return lax.rem(x + d, nx)
 
     def chain(g):
         xw, mw = xwin.at[g], mwin.at[g]
@@ -199,9 +200,18 @@
         yield
         arrive_rows(g, 0, xpick.at[g])
         apply(zhi, zlo, xpick.at[g], mpart.at[g])
-        copies = scatter(g, 1, mpart.at[g], mrecv.at[g])
-        yield
-        mw[1] = total(mpart.at[g], mrecv.at[g], copies)
+        copy = to_partner(g, 1, mpart.at[g], mpair.at[g])
+        yield
+        copy.wait_recv()
+        mhalf[g] = mpart[g, :, core] + mpair[g]
+        copies = [send(g, 6, d, mhalf.at[g, across(d)], mrecv.at[g, d - 1],
+                       2 * across(d) + core) for d in range(1, nx)]
+        yield
+        value = mhalf[g, x]
+        for d in range(1, nx):
+            copies[d - 1].wait_recv()
+            value = value + mrecv[g, d - 1]
+        mw[1] = value
         got = exchange(g, 1, mw.at[1], mw.at[1], mw.at[0], mw.at[2])
         yield
         got()
@@ -209,15 +219,25 @@
         yield
         arrive_rows(g, 2, mpick.at[g])
         apply(hhi, hlo, mpick.at[g], spart.at[g])
-        copies = scatter(g, 3, spart.at[g], srecv.at[g])
-        yield
-        whole = side.at[g]
-        whole[mine, :] = total(spart.at[g], srecv.at[g], copies)
-        for d in range(1, nc):
-            send(g, 4, d, whole.at[mine, :], whole.at[mine, :])
-        yield
-        arrive_rows(g, 4, whole)
-        apply(thi, tlo, whole, term.at[g])
+        copy = to_partner(g, 3, spart.at[g], spair.at[g])
+        yield
+        copy.wait_recv()
+        shalf[g] = spart[g, :, core] + spair[g]
+        copies = [send(g, 7, d, shalf.at[g], srecv.at[g, d - 1],
+                       2 * across(d) + core) for d in range(1, nx)]
+        yield
+        value = shalf[g]
+        for d in range(1, nx):
+            copies[d - 1].wait_recv()
+            value = value + srecv[g, d - 1]
+        side[g, :, core] = value
+        send(g, 4, 1, side.at[g, :, core], side.at[g, :, core], c + 1 - 2 * core)
+        yield
+        there = side.at[g, :, 1 - core]
+        pltpu.make_async_remote_copy(
+            there, there, peer_send.at[g, 4, 0], peer_recv.at[g, 4, 0],
+            device_id=(r, c + 1 - 2 * core), device_id_type=MESH).wait_recv()
+        apply(thi, tlo, side.at[g], term.at[g])
         copies = scatter(g, 5, term.at[g], trecv.at[g])
         yield
         sums = [jnp.zeros((sh, lanes), F32) for _ in range(3)]
@@ -263,7 +283,7 @@
     advance()
     for a in range(own):
         thi[a], tlo[a] = split(zf[a].T)
-    for _ in range(6):
+    for _ in range(8):
         advance()
     for copy in code_copies:
         copy.wait_send()
@@ -284,6 +304,8 @@
     dma = pltpu.SemaphoreType.DMA
     smem = pl.BlockSpec(memory_space=pltpu.SMEM)
     hbm = pl.BlockSpec(memory_space=pltpu.HBM)
+    nx = nc // 2
+    split_full, part = f(g, nx, 2, sh, lanes), f(g, nx, sh, lanes)
     full, peers, window = f(g, blk, lanes), f(g, nc - 1, sh, lanes), f(g, 3, sh, lanes)
     return pl.pallas_call(
         functools.partial(kernel, nr, nc, own, blk, width, w),
@@ -295,10 +317,11 @@
         ] + [halves] * 6 + [
             pltpu.VMEM((8, 128), jnp.int32), pltpu.VMEM((nc, 8, 128), jnp.int32),
             pltpu.SMEM((nc, 8, 128), jnp.int32),
-            full, window, peers, full, full, peers, window, peers, full,
-            full, peers, full, full, peers, window, f(g, 2, sh, lanes),
+            full, window, peers, full, split_full, f(g, nx - 1, sh, lanes), window, peers, full,
+            split_full, f(g, nx - 1, nx, sh, lanes), split_full, full, peers, window,
+            f(g, 2, sh, lanes), part, part, part, part,
             dma((3,)), dma, dma((nc - 1,)), dma((nc - 1,)),
-            dma((g, 6, nc - 1)), dma((g, 6, nc - 1)), dma((g, 3, 2)), dma((g, 3, 2)),
+            dma((g, 8, nc - 1)), dma((g, 8, nc - 1)), dma((g, 3, 2)), dma((g, 3, 2)),
         ],
         compiler_params=pltpu.CompilerParams(
             collective_id=0, has_side_effects=True, vmem_limit_bytes=60 * 1024 * 1024),

time: 42.2 us -> 41.6 us (0.986)
  Pallas kernels: 40.5 us -> 39.9 us
    pallas_call x1, Pallas kernels: 40.5 us -> 39.9 us  [local(): pl.pallas_call(functools.partial(kernel, nr, nc, own, blk, width, w), out...]
where the time goes in v3:
time: 41.6 us; the launch traced here: 41.4 us
  Pallas kernels  39.9 us (96%)
  local copies, waits for them, and re-layouts  1.57 us (4%)
    pallas_call x1, Pallas kernels, local(): pl.pallas_call(functools.partial(kernel, nr, nc, own, blk, width, w), out...  39.9 us
    unnamed x1, local copies, waits for them, and re-layouts  1.57 us

profile of v3, /device:TPU:0, one launch (start us, length us, event | category | flops | bytes accessed | tf_op | source)
XLA Modules:
  0.0 41.4 jit_solution(17589144281945329302)
XLA Ops:
  0.0 39.9 %shard_map.73 = f32[4,64,64]{2,1,0:T(8,128)} custom-call(s32[4]{0:T(128)} %bitcast.4, s32[4]{0:T(128)} %zn.1, s32[4]{0:T(128)} %bitcast.5, s32[4]{0:T(128)} %hn.1, f32[4,1,256,256]{3,2,1,0:T(8,128)} %z_hbm.1, f32[4,1,256,256]{3,2,1,0:T(8,128)} %h_hbm.1, f32[4,64,256]{2,1,0:T(8,128)} %bitcast.3), custom_call_target="tpu_custom_call" | custom-call | tf_op jit(solution)/shard_map/pallas_call | solution.py:310
  39.9 1.6 %copy.9 = f32[4,64,64]{2,1,0:T(8,128)} copy(f32[4,64,64]{2,1,0:T(8,128)} %shard_map.73) | data formatting | bytes 131072
